TPU v7x, 512 devices: a whole 4x8x8 slice. The times are simulated.
512 devices in a mesh: ctx: 64 (over z, x, core), head: 8 (over y).
Axes of the slice: x: 4, y: 8, z: 8, core: 2. Of those that a mesh axis runs over, the one named last changes fastest.
Arguments:
- hidden: bfloat16 [65536, 2048], P('ctx'), may hold values from -16 to 16
- qkv_weight: bfloat16 [2048, 3072], P('ctx', 'head'), may hold values from -0.125 to 0.125
- out_grad: float32 [65536, 1024], P('ctx', 'head'), may hold values from -6 to 6
Outputs:
- attended: float32 [65536, 1024], P('ctx', 'head')
- weight_grad: float32 [2048, 3072], P('ctx', 'head')
All inputs are finite; a program needn't handle non-finite values.
Results may differ from a plain program's by a relative error of at most 0.0018.
Values may be sent and summed in bfloat16 or wider, within the bound.
No kernel may reach another device: no remote copies, remote signals or barrier semaphores. Data moves between devices by JAX's collectives and lax.ppermute only.
A program may use at most 64 MiB of HBM per device.

v0:
```python
import jax
import jax.numpy as jnp
from jax import lax
from jax.sharding import PartitionSpec as P

HD = 128
BLOCK = 128
HIGH = lax.Precision.HIGHEST


def prefix_2(part, axis, combine, identity, reverse):
    count = lax.axis_size(axis)
    place = lax.axis_index(axis)
    ahead = count - 1 - place if reverse else place
    gathered = lax.all_gather(part, axis)
    state = jnp.zeros_like(part) + jnp.asarray(identity, part.dtype)

    def one(step, state):
        source = count - 1 - step if reverse else step
        return combine(state, lax.dynamic_index_in_dim(gathered, source, 0, False))

    return lax.fori_loop(0, ahead, one, state)


def local(hidden, qkv_weight, out_grad):
    tokens = hidden.shape[0]
    columns = qkv_weight.shape[1]
    heads = columns // (3 * HD)
    total_tokens = tokens * lax.axis_size("ctx")
    scale = float(HD * total_tokens) ** (-0.5)
    grad_scale = float(total_tokens) ** (-0.5)
    inputs = hidden
    proj = jnp.dot(
        inputs,
        lax.all_gather(qkv_weight, "ctx", axis=0, tiled=True),
        preferred_element_type=jnp.float32,
    )
    count = tokens // BLOCK
    proj = proj.reshape(count, BLOCK, heads, 3, HD)
    query = proj[:, :, :, 0]
    keys = proj[:, :, :, 1]
    values = proj[:, :, :, 2]
    cotangent = out_grad.reshape(count, BLOCK, heads, HD)
    kv_block = jnp.einsum("nshd,nshe->nhde", keys, values, precision=HIGH)
    qg_block = jnp.einsum("nthd,nthe->nhde", query, cotangent, precision=HIGH)
    kv_total = jnp.sum(kv_block, axis=0)
    qg_total = jnp.sum(qg_block, axis=0)
    zeros_state = jnp.zeros_like(kv_total)
    before = prefix_2(kv_total, "ctx", lambda a, b: a + b, zeros_state, False)
    after = prefix_2(qg_total, "ctx", lambda a, b: a + b, zeros_state, True)
    prefix = before[None] + jnp.cumsum(kv_block, axis=0) - kv_block
    suffix = after[None] + qg_total[None] - jnp.cumsum(qg_block, axis=0)
    rows = jnp.arange(BLOCK)
    mask = (rows[:, None] >= rows[None, :]).astype(jnp.float32)
    scores = jnp.einsum("nthd,nshd->nhts", query, keys, precision=HIGH) * mask
    inner = jnp.einsum("nhts,nshe->nthe", scores, values, precision=HIGH)
    carried = jnp.einsum("nthd,nhde->nthe", query, prefix, precision=HIGH)
    attended = (scale * (inner + carried)).reshape(tokens, heads * HD)
    dmat = jnp.einsum("nthe,nshe->nhts", cotangent, values, precision=HIGH) * mask
    dquery = scale * (
        jnp.einsum("nhts,nshd->nthd", dmat, keys, precision=HIGH)
        + jnp.einsum("nthe,nhde->nthd", cotangent, prefix, precision=HIGH)
    )
    dkeys = scale * (
        jnp.einsum("nhts,nthd->nshd", dmat, query, precision=HIGH)
        + jnp.einsum("nshe,nhde->nshd", values, suffix, precision=HIGH)
    )
    dvalues = scale * (
        jnp.einsum("nhts,nthe->nshe", scores, cotangent, precision=HIGH)
        + jnp.einsum("nshd,nhde->nshe", keys, suffix, precision=HIGH)
    )
    dproj = (
        jnp.stack([dquery, dkeys, dvalues], axis=3).reshape(tokens, columns).astype(jnp.bfloat16)
    )
    inputs = hidden
    product = lax.dot_general(
        inputs, dproj, (((0,), (0,)), ((), ())), preferred_element_type=jnp.float32
    )
    weight_grad = lax.psum_scatter(product * grad_scale, "ctx", scatter_dimension=0, tiled=True)
    return (attended, weight_grad)


def solution(mesh):
    return jax.shard_map(
        local,
        mesh=mesh,
        in_specs=(P("ctx", None), P("ctx", "head"), P("ctx", "head")),
        out_specs=(P("ctx", "head"), P("ctx", "head")),
        check_vma=False,
    )
```

profile of v0, /device:TPU:8, one launch (start us, length us, event | category | flops | bytes accessed | tf_op | source)
XLA Modules:
  0.0 499.1 jit_solution(4324925228339906326)
XLA Ops:
  8.0 91.0 %all-gather.6.cloned.1.call-done = bf16[2048,384]{1,0:T(8,128)(2,1)} async-done(((bf16[32,384]{1,0:T(8,128)(2,1)}), bf16[2048,384]{1,0:T(8,128)(2,1)}) %all-gather.6.cloned.1.call-update) | async-done | bytes 1572880 | tf_op jit(solution)/shard_map/all_gather | solution.py:35
  99.0 4.5 convolution_bitcast_fusion
  104.4 1.6 fusion.33
  106.4 2.5 fusion.34
  108.9 1.2 fusion.5
  110.2 1.8 fusion.22
  112.0 1.4 fusion.15
  113.4 1.2 convolution_multiply_fusion
  114.6 1.8 convolution_bitcast_fusion.1
  116.4 72.2 %all-gather.8.cloned.1.call-done = f32[8192,128]{1,0:T(8,128)} async-done(((f32[128,128]{1,0:T(8,128)}), f32[8192,128]{1,0:T(8,128)}) %all-gather.8.cloned.1.call-update) | async-done | bytes 4194320 | tf_op jit(solution)/shard_map/all_gather | solution.py:15
  188.6 85.3 %all-gather.10.cloned.1.call-done = f32[8192,128]{1,0:T(8,128)} async-done(((f32[128,128]{1,0:T(8,128)}), f32[8192,128]{1,0:T(8,128)}) %all-gather.10.cloned.1.call-update) | async-done | bytes 4194320 | tf_op jit(solution)/shard_map/all_gather | solution.py:15
  274.0 55.6 %while.23 = (s32[]{:T(128)}, f32[1,128,128]{2,1,0:T(8,128)S(1)}, s32[]{:T(128)}, f32[64,1,128,128]{3,2,1,0:T(8,128)}, s32[]{:T(128)}, /*index=5*/s32[]{:T(128)}, s32[]{:T(128)}, s32[]{:T(128)}) while((s32[]{:T(128)}, f32[1,128,128]{2,1,0:T(8,128)S(1)}, s32[]{:T(128)}, f32[64,1,128,128]{3,2,1,0:T(8,128)}, s32[]{:T(128)}, /*index=5*/s32[]{:T(128)}, ...), condition=%wide.region_6.7_spmd, body=%wide.region_5.6_spmd.sunk | while | flops 16390 | bytes 196751 | solution.py:22
  274.9 0.9 bitcast_add_fusion.6
  275.7 0.9 bitcast_add_fusion.6
  276.6 0.9 bitcast_add_fusion.6
  277.5 0.9 bitcast_add_fusion.6
  278.4 0.9 bitcast_add_fusion.6
  279.3 0.9 bitcast_add_fusion.6
  280.1 0.9 bitcast_add_fusion.6
  281.0 0.9 bitcast_add_fusion.6
  281.9 0.9 bitcast_add_fusion.6
  282.8 0.9 bitcast_add_fusion.6
  283.7 0.9 bitcast_add_fusion.6
  284.5 0.9 bitcast_add_fusion.6
  285.4 0.9 bitcast_add_fusion.6
  286.3 0.9 bitcast_add_fusion.6
  287.2 0.9 bitcast_add_fusion.6
  288.1 0.9 bitcast_add_fusion.6
  288.9 0.9 bitcast_add_fusion.6
  289.8 0.9 bitcast_add_fusion.6
  290.7 0.9 bitcast_add_fusion.6
  291.6 0.9 bitcast_add_fusion.6
  292.4 0.9 bitcast_add_fusion.6
  293.3 0.9 bitcast_add_fusion.6
  297.7 0.9 bitcast_add_fusion.6
  300.4 0.9 bitcast_add_fusion.6
  314.4 0.9 bitcast_add_fusion.6
  317.1 0.9 bitcast_add_fusion.6
  329.6 1.2 reduce-window_subtract_fusion
  330.8 1.7 fusion.9
  332.5 1.2 fusion.10
  333.7 1.2 fusion.11
  335.0 1.0 pad_maximum_fusion
  335.9 2.4 copy.58
  338.3 5.9 %multiply_bitcast_fusion = f32[2048,384]{0,1:T(8,128)} fusion(bf16[1024,2048]{1,0:T(8,128)(2,1)} %param.7, bf16[48,8,8,128]{3,2,1,0:T(8,128)(2,1)} %bitcast.117), kind=kOutput, calls=%fused_computation.2 | convolution fusion | flops 1611399168 | bytes 8126464 | tf_op jit(solution)/shard_map/dot_general | solution.py:76
  344.2 3.6 copy.73
  348.4 1.4 fusion.4
  349.8 142.7 %reduce-scatter.4.cloned.1.call-done = f32[32,384]{1,0:T(8,128)} async-done(((f32[2048,384]{1,0:T(8,128)}), f32[32,384]{1,0:T(8,128)}) %reduce-scatter.4.cloned.1.call-update) | async-done | bytes 49168
  (65 shorter events, 34.4 us)
Async XLA Ops:
  7.2 99.2 %copy-start = (f32[1024,128]{1,0:T(8,128)S(1)}, f32[1024,128]{1,0:T(8,128)}, u32[]{:S(2)}) copy-start(f32[1024,128]{1,0:T(8,128)} %param.9) | copy-start | bytes 1572868
  7.2 91.8 %all-gather.6.cloned.1.call-start = ((), (), s32[]{:S(2)}) async-start(), calls=%async_computation.1 | async-start | bytes 1597440 | tf_op jit(solution)/shard_map/all_gather | solution.py:35
  7.9 180.7 %all-gather.8.cloned.1.call-start = ((), (), s32[]{:S(2)}) async-start(), calls=%async_computation.2 | async-start | bytes 4259840 | tf_op jit(solution)/shard_map/all_gather | solution.py:15
  106.1 167.9 %all-gather.10.cloned.1.call-start = ((), (), s32[]{:S(2)}) async-start(), calls=%async_computation.3 | async-start | bytes 4259840 | tf_op jit(solution)/shard_map/all_gather | solution.py:15
  108.9 383.7 %reduce-scatter.4.cloned.1.call-start = ((), (), s32[]{:S(2)}) async-start(), calls=%async_computation.4 | async-start | bytes 3194880
  113.4 216.2 %copy-start.3 = (f32[128,128]{1,0:T(8,128)S(1)}, f32[128,128]{1,0:T(8,128)}, u32[]{:S(2)}) copy-start(f32[128,128]{1,0:T(8,128)} %get-tuple-element.122) | copy-start | bytes 196612
  329.6 2.9 copy-start.2
  329.6 4.1 copy-start.1
Sparse Core Ops, SparseCore 0:
  11.4 87.5 all-gather.5
  106.2 82.4 all-gather.7
  192.0 81.9 all-gather.9
  347.9 144.5 reduce-scatter.3
where the time goes:
time: 502 us; the launch traced here: 499 us
  waiting for transfers between devices  392 us (78%)
  other arithmetic  56.2 us (11%)
  matrix products  28.1 us (6%)
  between operations  13.9 us (3%)
  local copies, waits for them, and re-layouts  7.09 us (1%)
    all_gather x2, waiting for transfers between devices, prefix_2(): gathered = lax.all_gather(part, axis)  158 us
    unnamed x5, waiting for transfers between devices  143 us
    all_gather x1, waiting for transfers between devices, local(): lax.all_gather(qkv_weight, 'ctx', axis=0, tiled=True)  91 us
    add x63, other arithmetic, local(): after = prefix_2(qg_total, 'ctx', lambda a, b: a + b, zeros_state, True)  54 us
  transfers between devices with their start and end apart: 4, of which 4 were waited for; matrix products, arithmetic and copies ran while one was open for 2% of the time, Pallas kernels for 0%

commit v1 on v0

--- a/solution.py
+++ b/solution.py
@@ -32,7 +32,9 @@
     inputs = hidden
     proj = jnp.dot(
         inputs,
-        lax.all_gather(qkv_weight, "ctx", axis=0, tiled=True),
+        jnp.concatenate(
+            lax.all_to_all(jnp.stack([qkv_weight] * lax.axis_size("ctx")), "ctx", 0, 0), axis=0
+        ),
         preferred_element_type=jnp.float32,
     )
     count = tokens // BLOCK

time: 502 us -> 464 us (0.924)
  waiting for transfers between devices: 392 us -> 299 us
  blocking collectives: 0 us -> 53.7 us
    all_gather x1 -> x0, waiting for transfers between devices: 91 us -> none  [local(): lax.all_gather(qkv_weight, 'ctx', axis=0, tiled=True)]
    all_to_all x0 -> x1, blocking collectives: none -> 53.7 us  [local(): lax.all_to_all(jnp.stack([qkv_weight] * lax.axis_size('ctx')), 'ctx', 0, 0)]
    unnamed x5 -> x4, waiting for transfers between devices: 143 us -> 142 us
  transfers between devices with their start and end apart: 4 -> 3, of which waited for: 4 -> 3; matrix products, arithmetic and copies ran while one was open for 2% -> 3% of each run, Pallas kernels for 0% -> 0%
where the time goes in v1:
time: 464 us; the launch traced here: 461 us
  waiting for transfers between devices  299 us (64%)
  other arithmetic  56.2 us (12%)
  blocking collectives  53.7 us (12%)
  matrix products  27.1 us (6%)
  between operations  13.9 us (3%)
  local copies, waits for them, and re-layouts  9.72 us (2%)
    all_gather x2, waiting for transfers between devices, prefix_2(): gathered = lax.all_gather(part, axis)  157 us
    unnamed x4, waiting for transfers between devices  142 us
    add x63, other arithmetic, local(): after = prefix_2(qg_total, 'ctx', lambda a, b: a + b, zeros_state, True)  54 us
    all_to_all x1, blocking collectives, local(): lax.all_to_all(jnp.stack([qkv_weight] * lax.axis_size('ctx')), 'ctx', 0, 0)  53.7 us
  transfers between devices with their start and end apart: 3, of which 3 were waited for; matrix products, arithmetic and copies ran while one was open for 3% of the time, Pallas kernels for 0%

profile of v1, /device:TPU:8, one launch (start us, length us, event | category | flops | bytes accessed | tf_op | source)
XLA Modules:
  0.0 461.3 jit_solution(3566302659330294318)
XLA Ops:
  7.2 0.9 stack.14
  8.1 53.7 %all_to_all.5 = bf16[64,32,384]{2,1,0:T(8,128)(2,1)S(1)} all-to-all(bf16[64,32,384]{2,1,0:T(8,128)(2,1)S(1)} %stack.14), channel_id=1, replica_groups=mesh['ctx'=64,'head'=8] {'ctx'}, dimensions={0} | all-to-all | bytes 3145728 | tf_op jit(solution)/shard_map/all_to_all | solution.py:36
  61.9 1.6 copy.36
  63.5 4.6 convolution_bitcast_fusion
  68.1 1.6 fusion.20
  69.8 2.5 fusion.21
  72.4 1.2 fusion.5
  73.6 1.8 fusion.17
  75.4 1.4 fusion.18
  76.8 1.2 convolution_multiply_fusion
  78.1 1.8 convolution_bitcast_fusion.1
  79.9 71.3 %all-gather.5.cloned.1.call-done = f32[8192,128]{1,0:T(8,128)} async-done(((f32[128,128]{1,0:T(8,128)}), f32[8192,128]{1,0:T(8,128)}) %all-gather.5.cloned.1.call-update) | async-done | bytes 4194320 | tf_op jit(solution)/shard_map/all_gather | solution.py:15
  151.2 85.3 %all-gather.7.cloned.1.call-done = f32[8192,128]{1,0:T(8,128)} async-done(((f32[128,128]{1,0:T(8,128)}), f32[8192,128]{1,0:T(8,128)}) %all-gather.7.cloned.1.call-update) | async-done | bytes 4194320 | tf_op jit(solution)/shard_map/all_gather | solution.py:15
  236.5 55.6 %while.23 = (s32[]{:T(128)}, f32[1,128,128]{2,1,0:T(8,128)S(1)}, s32[]{:T(128)}, f32[64,1,128,128]{3,2,1,0:T(8,128)}, s32[]{:T(128)}, /*index=5*/s32[]{:T(128)}, s32[]{:T(128)}, s32[]{:T(128)}) while((s32[]{:T(128)}, f32[1,128,128]{2,1,0:T(8,128)S(1)}, s32[]{:T(128)}, f32[64,1,128,128]{3,2,1,0:T(8,128)}, s32[]{:T(128)}, /*index=5*/s32[]{:T(128)}, ...), condition=%wide.region_6.7_spmd, body=%wide.region_5.6_spmd.sunk | while | flops 16390 | bytes 196751 | solution.py:22
  237.4 0.9 bitcast_add_fusion.6
  238.2 0.9 bitcast_add_fusion.6
  239.1 0.9 bitcast_add_fusion.6
  240.0 0.9 bitcast_add_fusion.6
  240.9 0.9 bitcast_add_fusion.6
  241.8 0.9 bitcast_add_fusion.6
  242.6 0.9 bitcast_add_fusion.6
  243.5 0.9 bitcast_add_fusion.6
  244.4 0.9 bitcast_add_fusion.6
  245.3 0.9 bitcast_add_fusion.6
  246.2 0.9 bitcast_add_fusion.6
  247.0 0.9 bitcast_add_fusion.6
  247.9 0.9 bitcast_add_fusion.6
  248.8 0.9 bitcast_add_fusion.6
  249.7 0.9 bitcast_add_fusion.6
  250.6 0.9 bitcast_add_fusion.6
  251.4 0.9 bitcast_add_fusion.6
  252.3 0.9 bitcast_add_fusion.6
  253.2 0.9 bitcast_add_fusion.6
  254.1 0.9 bitcast_add_fusion.6
  254.9 0.9 bitcast_add_fusion.6
  261.1 0.9 bitcast_add_fusion.6
  263.7 0.9 bitcast_add_fusion.6
  277.8 0.9 bitcast_add_fusion.6
  280.5 0.9 bitcast_add_fusion.6
  292.1 1.2 reduce-window_subtract_fusion
  293.9 1.2 fusion.10
  296.0 1.2 fusion.11
  297.2 1.0 pad_maximum_fusion
  298.2 2.4 copy.50
  300.6 5.9 %multiply_bitcast_fusion = f32[2048,384]{0,1:T(8,128)} fusion(bf16[1024,2048]{1,0:T(8,128)(2,1)} %param.7, bf16[48,8,8,128]{3,2,1,0:T(8,128)(2,1)} %bitcast.116), kind=kOutput, calls=%fused_computation.2 | convolution fusion | flops 1611399168 | bytes 8126464 | tf_op jit(solution)/shard_map/dot_general | solution.py:78
  306.5 3.6 copy.65
  311.1 1.4 fusion.4
  312.5 142.3 %reduce-scatter.4.cloned.1.call-done = f32[32,384]{1,0:T(8,128)} async-done(((f32[2048,384]{1,0:T(8,128)}), f32[32,384]{1,0:T(8,128)}) %reduce-scatter.4.cloned.1.call-update) | async-done | bytes 49168
  (66 shorter events, 35.3 us)
Async XLA Ops:
  7.2 62.7 %copy-start = (f32[1024,128]{1,0:T(8,128)S(1)}, f32[1024,128]{1,0:T(8,128)}, u32[]{:S(2)}) copy-start(f32[1024,128]{1,0:T(8,128)} %param.9) | copy-start | bytes 1572868
  7.2 144.0 %all-gather.5.cloned.1.call-start = ((), (), s32[]{:S(2)}) async-start(), calls=%async_computation.2 | async-start | bytes 4259840 | tf_op jit(solution)/shard_map/all_gather | solution.py:15
  69.8 166.7 %all-gather.7.cloned.1.call-start = ((), (), s32[]{:S(2)}) async-start(), calls=%async_computation.3 | async-start | bytes 4259840 | tf_op jit(solution)/shard_map/all_gather | solution.py:15
  72.3 382.4 %reduce-scatter.4.cloned.1.call-start = ((), (), s32[]{:S(2)}) async-start(), calls=%async_computation.4 | async-start | bytes 3194880
  79.9 212.2 %copy-start.6 = (f32[128,128]{1,0:T(8,128)S(1)}, f32[128,128]{1,0:T(8,128)}, u32[]{:S(2)}) copy-start(f32[128,128]{1,0:T(8,128)} %get-tuple-element.119) | copy-start | bytes 196612
  292.1 1.2 copy-start.5
  292.1 1.8 copy-start.4
  293.9 2.1 copy-start.3
  295.2 0.8 copy-start.1
  310.0 1.0 copy-start.2
Sparse Core Ops, SparseCore 0:
  69.9 81.2 all-gather.4
  154.5 81.9 all-gather.6
  310.2 144.5 reduce-scatter.3
